TPU v7x, 128 devices: a whole 4x4x4 slice. The times are simulated.
128 devices in a mesh: seq: 8 (over z, core), head: 16 (over y, x).
Axes of the slice: x: 4, y: 4, z: 4, core: 2. Of those that a mesh axis runs over, the one named last changes fastest.
Arguments:
- queries: bfloat16 [32768, 4096], P(('seq', 'head')), may hold values from -8 to 8
- keys: bfloat16 [32768, 4096], P(('seq', 'head')), may hold values from -8 to 8
- values: bfloat16 [32768, 4096], P(('seq', 'head')), may hold values from -6 to 6
- head_kind: int32 [32], replicated, may hold values 0 or 1
Outputs:
- attended: bfloat16 [32768, 4096], P(('seq', 'head'))
All inputs are finite; a program needn't handle non-finite values.
Results may differ from a plain program's by a relative error of at most 0.012.
Values may be sent and summed in bfloat16 or wider, within the bound.
No kernel may reach another device: no remote copies, remote signals or barrier semaphores. Data moves between devices by JAX's collectives and lax.ppermute only.
A program may use at most 128 MiB of HBM per device.

v0:
```python
import functools

import jax
import jax.numpy as jnp
from jax import lax
from jax.experimental import pallas as pl
from jax.experimental.pallas import tpu as pltpu
from jax.sharding import Mesh, PartitionSpec as P

HEAD_DIM = 128
P_SIZE = 2048
HEADS = 32
ROWS = 256
RANKS = 8
FRAMES = 16
SCALE = HEAD_DIM**-0.5
LOG2E = 1.4426950408889634
SAFE = 60.0
FRAME_GROUP = ("yl", "x")
BLOCK_GROUP = ("yh", "yl", "x")
SPOT_GROUP = ("z", "c", "yh")
VMEM = 48 * 1024 * 1024

CASES = ((1, 0, 20), (1, 1, 16), (1, 0, 32), (2, 0, 8))


def order_heads(kind_ref, order_ref):
    spatial = lax.fori_loop(0, HEADS, lambda h, n: n + 1 - kind_ref[h], jnp.int32(0))

    def place(h, counts):
        a, b = counts
        kind = kind_ref[h]
        order_ref[jnp.where(kind == 0, a, b)] = h
        return a + 1 - kind, b + kind

    lax.fori_loop(0, HEADS, place, (jnp.int32(0), spatial))
    return spatial


def columns(slot):
    if isinstance(slot, int):
        return pl.ds(slot * HEAD_DIM, HEAD_DIM)
    return pl.ds(pl.multiple_of(slot * HEAD_DIM, HEAD_DIM), HEAD_DIM)


def start_columns(part, width, groups, source, target, head_of, sem):
    def each(act):
        @pl.loop(0, groups)
        def _(group):
            for place in range(width):
                head = head_of(place * groups + group)
                copy = pltpu.make_async_copy(
                    source.at[:, columns(head)],
                    target.at[group, :, columns(part * width + place)],
                    sem.at[group * width + place],
                )
                getattr(copy, act)()

    each("start")
    return lambda: each("wait")


def pack_kernel(plan, n_out, kind_ref, q_ref, k_ref, v_ref, *refs):
    outs, order_ref, sems = refs[:n_out], refs[n_out], refs[n_out + 1 :]
    spatial = order_heads(kind_ref, order_ref)
    sources = {"q": q_ref, "k": k_ref, "v": v_ref}
    waits = []
    for sem, (out, part, width, base, groups, name) in zip(sems, plan):

        def head_of(slot, base=base):
            if base is None:
                return order_ref[jnp.minimum(spatial + slot, HEADS - 1)]
            return order_ref[base + slot]

        waits.append(start_columns(part, width, groups, sources[name], outs[out], head_of, sem))
    for wait in waits:
        wait()


def pack(plan, shapes, head_kind, queries, keys, values):
    outs = tuple(jax.ShapeDtypeStruct(shape, jnp.bfloat16) for shape in shapes)
    return pl.pallas_call(
        functools.partial(pack_kernel, plan, len(shapes)),
        out_shape=outs,
        in_specs=[pl.BlockSpec(memory_space=pltpu.SMEM)] + [pl.BlockSpec(memory_space=pl.ANY)] * 3,
        out_specs=(pl.BlockSpec(memory_space=pltpu.VMEM),) * len(shapes),
        scratch_shapes=[pltpu.SMEM((HEADS,), jnp.int32)]
        + [pltpu.SemaphoreType.DMA((width * groups,)) for _, _, width, _, groups, _ in plan],
        compiler_params=pltpu.CompilerParams(vmem_limit_bytes=VMEM),
        name="pack",
    )(head_kind, queries, keys, values)


def unpack_kernel(layouts, ct, kind_ref, *refs):
    s_refs, (t_ref, out_ref, order_ref, sems) = refs[: len(layouts)], refs[len(layouts) :]
    spatial = order_heads(kind_ref, order_ref)

    def target(slot):
        return out_ref.at[:, columns(order_ref[slot])]

    for (width, base, groups), ref in zip(layouts, s_refs):

        @pl.loop(0, groups)
        def _(group):
            for place in range(width):
                slot = base + place * groups + group
                source = ref.at[group, :, columns(place)]
                copy = pltpu.make_async_copy(source, target(slot), sems.at[slot])
                pl.when(slot < spatial)(copy.start)

    def from_t(slot):
        source = t_ref.at[:, columns(jnp.clip(slot - spatial, 0, ct - 1))]
        return pltpu.make_async_copy(source, target(slot), sems.at[slot])

    @pl.loop(spatial, HEADS)
    def _(slot):
        from_t(slot).start()

    @pl.loop(0, HEADS)
    def _(slot):
        from_t(slot).wait()


def unpack(layouts, ct, head_kind, s_backs, t_back):
    n = len(layouts)
    return pl.pallas_call(
        functools.partial(unpack_kernel, layouts, ct),
        out_shape=jax.ShapeDtypeStruct((ROWS, HEADS * HEAD_DIM), jnp.bfloat16),
        in_specs=[pl.BlockSpec(memory_space=pltpu.SMEM)]
        + [pl.BlockSpec(memory_space=pltpu.VMEM)] * (n + 1),
        out_specs=pl.BlockSpec(memory_space=pl.ANY),
        scratch_shapes=[pltpu.SMEM((HEADS,), jnp.int32), pltpu.SemaphoreType.DMA((HEADS,))],
        compiler_params=pltpu.CompilerParams(vmem_limit_bytes=VMEM),
        name="unpack",
    )(head_kind, *s_backs, t_back)


def dot_t(a, b):
    return lax.dot_general(a, b, (((1,), (1,)), ((), ())), preferred_element_type=jnp.float32)


def higher_norm2(best, x):
    wide = x.astype(jnp.float32)
    return jnp.maximum(best, jnp.sum(wide * wide, axis=-1, keepdims=True))


BQ = 1024
STEP = 1024
BK = 256


def spatial_unit(first_ref, q_ref, k_ref, v_ref, k0_ref, v0_ref, o_ref, kext, vext, total, norm):
    first = jnp.logical_and(first_ref[0] == 1, pl.program_id(1) == 0)

    step = pl.program_id(2)
    none = jnp.zeros((ROWS, 1), jnp.float32)

    @pl.when(pl.program_id(0) + pl.program_id(1) + step == 0)
    def _():
        vext[:, HEAD_DIM:] = jnp.ones((2 * P_SIZE, HEAD_DIM), jnp.bfloat16)

    @pl.when(step == 0)
    def _():
        def load(rank, best):
            own = pl.ds(pl.multiple_of(rank * ROWS, ROWS), ROWS)
            zero = pl.ds(pl.multiple_of(P_SIZE + rank * ROWS, ROWS), ROWS)
            kext[own], kext[zero] = k_ref[rank], k0_ref[rank]
            vext[own, :HEAD_DIM], vext[zero, :HEAD_DIM] = v_ref[rank], v0_ref[rank]
            return higher_norm2(higher_norm2(best, k_ref[rank]), k0_ref[rank])

        norm[0] = jnp.max(lax.fori_loop(0, RANKS, load, none))

    q = q_ref[...].reshape(BQ, HEAD_DIM)
    longest = lax.fori_loop(0, BQ // ROWS, lambda i, best: higher_norm2(best, q_ref[i]), none)
    small = norm[0] * jnp.max(longest) * (SCALE * SCALE) <= SAFE * SAFE
    factor = SCALE * LOG2E
    keys = jnp.where(first, P_SIZE, 2 * P_SIZE)

    def block(ref, start, size):
        return ref[pl.ds(pl.multiple_of(start, size), size)]

    total[...] = jnp.zeros_like(total)

    @pl.when(small)
    def _():
        @pl.loop(0, keys // STEP)
        def _(turn):
            for b in range(STEP // BK):
                start = turn * STEP + b * BK
                scores = dot_t(q, block(kext, start, BK))
                weights = jnp.exp2(scores * factor).astype(jnp.bfloat16)
                total[...] += jnp.dot(
                    weights, block(vext, start, BK), preferred_element_type=jnp.float32
                )

    @pl.when(jnp.logical_not(small))
    def _():
        @pl.loop(0, BQ // ROWS)
        def _(part):
            rows = q_ref[part]

            def highest(turn, top):
                scores = dot_t(rows, block(kext, turn * ROWS, ROWS))
                return jnp.maximum(top, jnp.max(scores, axis=-1, keepdims=True))

            lowest = jnp.full((ROWS, 1), -jnp.inf, jnp.float32)
            top = lax.fori_loop(0, keys // ROWS, highest, lowest)

            def add(turn, held):
                scores = dot_t(rows, block(kext, turn * ROWS, ROWS))
                weights = jnp.exp2((scores - top) * factor).astype(jnp.bfloat16)
                values = block(vext, turn * ROWS, ROWS)
                return held + jnp.dot(weights, values, preferred_element_type=jnp.float32)

            held = jnp.zeros((ROWS, 2 * HEAD_DIM), jnp.float32)
            held = lax.fori_loop(0, keys // ROWS, add, held)
            total[pl.ds(pl.multiple_of(part * ROWS, ROWS), ROWS)] = held

    out = total[:, :HEAD_DIM] / total[:, HEAD_DIM:]
    o_ref[...] = out.astype(jnp.bfloat16).reshape(o_ref.shape)


def spatial_kernel(first_ref, *refs):
    pl.when(pl.program_id(0) < first_ref[1])(lambda: spatial_unit(first_ref, *refs))


def spatial_attention(width, frames, first, q, kv, keys_at, kv0):
    whole = (RANKS, ROWS, HEAD_DIM)
    part = (BQ // ROWS, ROWS, HEAD_DIM)
    steps = P_SIZE // BQ
    grid_spec = pltpu.PrefetchScalarGridSpec(
        num_scalar_prefetch=1,
        grid=(width, frames, steps),
        in_specs=[
            pl.BlockSpec(part, lambda j, u, g, first: (u * steps + g, 0, j)),
            pl.BlockSpec(whole, lambda j, u, g, first: (u, 0, keys_at + j)),
            pl.BlockSpec(whole, lambda j, u, g, first: (u, 0, keys_at + width + j)),
            pl.BlockSpec(whole, lambda j, u, g, first: (0, 0, j)),
            pl.BlockSpec(whole, lambda j, u, g, first: (0, 0, j)),
        ],
        out_specs=pl.BlockSpec(part, lambda j, u, g, first: (u * steps + g, 0, j)),
        scratch_shapes=[
            pltpu.VMEM((2 * P_SIZE, HEAD_DIM), jnp.bfloat16),
            pltpu.VMEM((2 * P_SIZE, 2 * HEAD_DIM), jnp.bfloat16),
            pltpu.VMEM((BQ, 2 * HEAD_DIM), jnp.float32),
            pltpu.SMEM((1,), jnp.float32),
        ],
    )
    units = width * frames
    return pl.pallas_call(
        spatial_kernel,
        grid_spec=grid_spec,
        out_shape=jax.ShapeDtypeStruct((frames * RANKS, ROWS, width * HEAD_DIM), jnp.bfloat16),
        compiler_params=pltpu.CompilerParams(vmem_limit_bytes=VMEM),
        cost_estimate=pl.CostEstimate(
            flops=units * 2**26,
            bytes_accessed=units * 2**16,
            transcendentals=units * 2**16,
        ),
        name="spatial",
    )(first, q, kv, kv, *kv0)


SPOTS = ROWS // FRAMES
PER_STEP = 4


def temporal_kernel(q_ref, k_ref, v_ref, o_ref):
    row = lax.broadcasted_iota(jnp.int32, (ROWS, ROWS), 0)
    col = lax.broadcasted_iota(jnp.int32, (ROWS, ROWS), 1)
    same = (row & (SPOTS - 1)) == (col & (SPOTS - 1))
    for h in range(PER_STEP):
        cols = slice(h * HEAD_DIM, (h + 1) * HEAD_DIM)
        q, k, v = (ref[:, :, cols].reshape(ROWS, HEAD_DIM) for ref in (q_ref, k_ref, v_ref))
        scores = jnp.where(same, dot_t(q, k) * (SCALE * LOG2E), -1e30)
        top = jnp.max(scores, axis=-1, keepdims=True)
        weights = jnp.exp2(scores - top)
        total = jnp.sum(weights, axis=-1, keepdims=True)
        out = jnp.dot(weights.astype(jnp.bfloat16), v, preferred_element_type=jnp.float32) / total
        o_ref[:, :, cols] = out.astype(jnp.bfloat16).reshape(FRAMES, SPOTS, HEAD_DIM)


def temporal_attention(ct, qkv):
    block = (FRAMES, SPOTS, PER_STEP * HEAD_DIM)
    steps = ct // PER_STEP
    return pl.pallas_call(
        temporal_kernel,
        grid=(steps,),
        in_specs=[
            pl.BlockSpec(block, lambda h: (0, 0, h)),
            pl.BlockSpec(block, lambda h: (0, 0, steps + h)),
            pl.BlockSpec(block, lambda h: (0, 0, 2 * steps + h)),
        ],
        out_specs=pl.BlockSpec(block, lambda h: (0, 0, h)),
        out_shape=jax.ShapeDtypeStruct((FRAMES, SPOTS, ct * HEAD_DIM), jnp.bfloat16),
        compiler_params=pltpu.CompilerParams(vmem_limit_bytes=VMEM),
        cost_estimate=pl.CostEstimate(
            flops=ct * 256 * 256 * 128 * 4,
            bytes_accessed=ct * 2**18,
            transcendentals=ct * 256 * 256,
        ),
        name="temporal",
    )(qkv, qkv, qkv)


def exchange(x, group):
    return lax.all_to_all(x, group, split_axis=0, concat_axis=0, tiled=True)


def spot(z, c, yh):
    return z * 4 + c * 2 + yh


def send(x, pairs):
    return lax.ppermute(x, SPOT_GROUP, [(spot(*a), spot(*b)) for a, b in pairs])


def along_z(kv, halves):
    z = lax.axis_index("z")
    z1, z3, z2 = (send(kv, [((0, 0, h), (i, 0, h)) for h in halves]) for i in (1, 3, 2))
    return jnp.where(z == 0, kv, jnp.where(z == 1, z1, jnp.where(z == 2, z2, z3)))


def along_y(ring):
    across = send(ring, [((i, 0, 0), (i, 0, 1)) for i in range(4)])
    return jnp.where(lax.axis_index("yh") == 0, ring, across)


def to_core(ring):
    pairs = [((i, 0, h), (i, 1, h)) for i in range(4) for h in range(2)]
    cols = ring.shape[2] // 2
    own = lax.axis_index("c") == 0
    return [jnp.where(own, x, send(x, pairs)) for x in (ring[:, :, :cols], ring[:, :, cols:])]


def attend(a, b, ct, queries, keys, values, head_kind):
    z, c, yh = (lax.axis_index(name) for name in SPOT_GROUP)
    arrays = (head_kind, queries, keys, values)
    wide, narrow = 2 * RANKS, RANKS
    spatial = HEADS - jnp.sum(head_kind)

    def unit(first, base, group, groups, width):
        held = (spatial - base - lax.axis_index(group) + groups - 1) // groups
        return jnp.stack([first.astype(jnp.int32), jnp.clip(held, 0, width)])

    if b:
        base = a * wide
        plan = [(0, part, b, base, narrow, name) for part, name in enumerate("qkv")]
        (qkv_send,) = pack(plan, [(narrow, ROWS, 3 * b * HEAD_DIM)], *arrays)
        qkv_b = exchange(qkv_send, FRAME_GROUP)

    plan = [(0, part, a, 0, wide, name) for part, name in enumerate("kv")]
    (kv_send,) = pack(plan, [(wide, ROWS, 2 * a * HEAD_DIM)], *arrays)
    if b:
        qkv_b, kv_send = lax.optimization_barrier((qkv_b, kv_send))
    kv_a = exchange(kv_send, BLOCK_GROUP)
    if b:
        ring_b = along_y(along_z(qkv_b[:, :, b * HEAD_DIM :], (0,)))

    plan = [(0, 0, a, 0, wide, "q")]
    plan += [(1, part, ct, None, 1, name) for part, name in enumerate("qkv")]
    shapes = [(wide, ROWS, a * HEAD_DIM), (1, ROWS, 3 * ct * HEAD_DIM)]
    q_send, t_send = pack(plan, shapes, *arrays)
    kv_a, q_send = lax.optimization_barrier((kv_a, q_send))
    q_a = exchange(q_send, BLOCK_GROUP)
    ring_a = along_z(kv_a[:RANKS], (0, 1))

    t_send = t_send.reshape(FRAMES, SPOTS, 3 * ct * HEAD_DIM)
    if b:
        q_a, ring_a, ring_b, t_send = lax.optimization_barrier((q_a, ring_a, ring_b, t_send))
    else:
        q_a, ring_a, t_send = lax.optimization_barrier((q_a, ring_a, t_send))
    t_have = exchange(t_send, SPOT_GROUP)

    backs, layouts = [], []
    if b:
        at = unit(z + c + yh == 0, a * wide, FRAME_GROUP, narrow, b)
        out = spatial_attention(b, 1, at, qkv_b, qkv_b, b, to_core(ring_b))
        out, t_have = lax.optimization_barrier((out, t_have))
        backs.append(exchange(out, FRAME_GROUP))
        layouts.append((b, a * wide, narrow))
    at = unit(z + c == 0, 0, BLOCK_GROUP, wide, a)
    out = spatial_attention(a, 2, at, q_a, kv_a, 0, to_core(ring_a))
    backs.append(exchange(out, BLOCK_GROUP))
    layouts.append((a, 0, wide))
    t_out = temporal_attention(ct, t_have)
    t_back = exchange(t_out, SPOT_GROUP).reshape(ROWS, ct * HEAD_DIM)
    return unpack(layouts, ct, head_kind, backs, t_back)


def on_device(queries, keys, values, head_kind):
    temporal = jnp.sum(head_kind)
    spatial = HEADS - temporal
    index = jnp.int32(len(CASES) - 1)
    for i in reversed(range(len(CASES))):
        a, b, ct = CASES[i]
        room = 2 * RANKS * a + RANKS * b
        index = jnp.where(jnp.logical_and(spatial <= room, temporal <= ct), i, index)
    branches = [functools.partial(attend, *case) for case in CASES]
    return lax.switch(index, branches, queries, keys, values, head_kind)


def solution(mesh):
    fine = Mesh(mesh.devices.reshape(4, 2, 2, 2, 4), ("z", "c", "yh", "yl", "x"))
    rows = P(("z", "c", "yh", "yl", "x"), None)
    return jax.shard_map(
        on_device, mesh=fine, in_specs=(rows, rows, rows, P()), out_specs=rows, check_vma=False
    )
```

profile of v0, /device:TPU:97, one launch (start us, length us, event | category | flops | bytes accessed | tf_op | source)
XLA Modules:
  0.0 317.0 jit_solution(18304762558564473927)
XLA Ops:
  3.9 312.9 %conditional.1 = (bf16[256,4096]{1,0:T(8,128)(2,1)}) conditional(s32[]{:T(128)} %clamp.3, (s32[32]{0:T(128)}, bf16[256,4096]{1,0:T(8,128)(2,1)}, bf16[256,4096]{1,0:T(8,128)(2,1)}, bf16[256,4096]{1,0:T(8,128)(2,1)}) %tuple.27, (s32[32]{0:T(128)}, bf16[256,4096]{1,0:T(8,128)(2,1)}, bf16[256,4096]{1,0:T(8,128)(2,1)}, ...), branch_computations={%region_1.3_spmd, %region_3.5_spmd, %region_5.7_spmd, %region_7.9_... | conditional | flops 1210056832 | bytes 178456992 | solution.py:400
  3.9 3.2 pack.9
  7.1 1.3 copy-done.4
  8.4 6.9 %all-to-all-start = ((bf16[16,256,256]{2,1,0:T(8,128)(2,1)}), bf16[16,256,256]{2,1,0:T(8,128)(2,1)S(1)}, u32[]{:S(2)}, u32[]{:S(2)}) async-start(bf16[16,256,256]{2,1,0:T(8,128)(2,1)} %copy-done.4), calls=%async_computation | async-start | bytes 4194304 | tf_op jit(solution)/shard_map/cond/branch_0_fun/all_to_all | solution.py:307
  15.3 4.4 %pack.10 = (bf16[16,256,128]{2,1,0:T(8,128)(2,1)S(1)}, bf16[1,256,7680]{2,1,0:T(8,128)(2,1)S(1)}) custom-call(s32[32]{0:T(128)S(1)} %copy-done.26, bf16[256,4096]{1,0:T(8,128)(2,1)} %get-tuple-element.104.q_ref, bf16[256,4096]{1,0:T(8,128)(2,1)} %get-tuple-element.108.k_ref, bf16[256,4096]{1,0:T(8,128)(2,1)} %get-tuple-element.112.v_ref), custom_call_target="tpu_custom_call" | custom-call | tf_op jit(solution)/shard_map/cond/branch_0_fun/pack/pallas_call | solution.py:82
  19.7 1.9 copy-done.12
  22.6 23.2 %all-to-all-done.refs_1_.refs_2_ = bf16[16,256,256]{2,1,0:T(8,128)(2,1)S(1)} async-done(((bf16[16,256,256]{2,1,0:T(8,128)(2,1)}), bf16[16,256,256]{2,1,0:T(8,128)(2,1)S(1)}, u32[]{:S(2)}, u32[]{:S(2)}) %all-to-all-start) | async-done | bytes 2097184 | tf_op jit(solution)/shard_map/cond/branch_0_fun/all_to_all | solution.py:307
  46.8 1.7 collective-permute-start
  48.5 1.7 collective-permute-start.1
  50.2 1.7 collective-permute-start.2
  51.9 4.3 %all-to-all-start.1 = ((bf16[16,256,128]{2,1,0:T(8,128)(2,1)}), bf16[16,256,128]{2,1,0:T(8,128)(2,1)S(1)}, u32[]{:S(2)}, u32[]{:S(2)}) async-start(bf16[16,256,128]{2,1,0:T(8,128)(2,1)} %copy-done.19), calls=%async_computation.1 | async-start | bytes 2097152 | tf_op jit(solution)/shard_map/cond/branch_0_fun/all_to_all | solution.py:307
  56.2 2.4 select_select_fusion
  58.6 13.5 %all-to-all-done.1.refs_0_ = bf16[16,256,128]{2,1,0:T(8,128)(2,1)S(1)} async-done(((bf16[16,256,128]{2,1,0:T(8,128)(2,1)}), bf16[16,256,128]{2,1,0:T(8,128)(2,1)S(1)}, u32[]{:S(2)}, u32[]{:S(2)}) %all-to-all-start.1) | async-done | bytes 1048608 | tf_op jit(solution)/shard_map/cond/branch_0_fun/all_to_all | solution.py:307
  72.1 11.3 %all-to-all-start.3 = ((bf16[16,16,7680]{2,1,0:T(8,128)(2,1)}), bf16[16,16,7680]{2,1,0:T(8,128)(2,1)}, u32[]{:S(2)}, u32[]{:S(2)}) async-start(bf16[16,16,7680]{2,1,0:T(8,128)(2,1)} %bitcast.21), calls=%async_computation.3 | async-start | bytes 7864320 | tf_op jit(solution)/shard_map/cond/branch_0_fun/all_to_all | solution.py:307
  83.4 1.9 slice.32
  86.6 2.8 collective-permute-done.4
  89.4 2.4 broadcast_select_fusion
  94.5 1.4 collective-permute-done.3
  98.3 167.5 %spatial.5 = bf16[16,256,128]{2,1,0:T(8,128)(2,1)S(1)} custom-call(s32[2]{0:T(128)S(1)} %pad_add_fusion.first_ref, bf16[16,256,128]{2,1,0:T(8,128)(2,1)S(1)} %all-to-all-done.1.refs_0_, bf16[16,256,256]{2,1,0:T(8,128)(2,1)S(1)} %all-to-all-done.refs_1_.refs_2_, bf16[16,256,256]{2,1,0:T(8,128)(2,1)S(1)} %all-to-all-done.refs_1_.refs_2_, ...), custom_call_target="tpu_custom_call" | custom-call | flops 134217728 | bytes 131072 | tf_op jit(solution)/shard_map/cond/branch_0_fun/spatial/pallas_call | solution.py:250
  266.7 5.4 %all-to-all-start.2 = ((bf16[16,256,128]{2,1,0:T(8,128)(2,1)}), bf16[16,256,128]{2,1,0:T(8,128)(2,1)S(1)}, u32[]{:S(2)}, u32[]{:S(2)}) async-start(bf16[16,256,128]{2,1,0:T(8,128)(2,1)} %copy-done.10), calls=%async_computation.2 | async-start | bytes 2097152 | tf_op jit(solution)/shard_map/cond/branch_0_fun/all_to_all | solution.py:307
  272.1 5.9 %temporal.4 = bf16[16,16,2560]{2,1,0:T(8,128)(2,1)S(1)} custom-call(bf16[16,16,7680]{2,1,0:T(8,128)(2,1)} %all-to-all-done.3.q_ref.k_ref.v_ref, bf16[16,16,7680]{2,1,0:T(8,128)(2,1)} %all-to-all-done.3.q_ref.k_ref.v_ref, bf16[16,16,7680]{2,1,0:T(8,128)(2,1)} %all-to-all-done.3.q_ref.k_ref.v_ref), custom_call_target="tpu_custom_call" | custom-call | flops 671088640 | bytes 5242880 | tf_op jit(solution)/shard_map/cond/branch_0_fun/temporal/pallas_call | solution.py:286
  278.1 10.4 %all-to-all-done.2.refs_0_ = bf16[16,256,128]{2,1,0:T(8,128)(2,1)S(1)} async-done(((bf16[16,256,128]{2,1,0:T(8,128)(2,1)}), bf16[16,256,128]{2,1,0:T(8,128)(2,1)S(1)}, u32[]{:S(2)}, u32[]{:S(2)}) %all-to-all-start.2) | async-done | bytes 1048608 | tf_op jit(solution)/shard_map/cond/branch_0_fun/all_to_all | solution.py:307
  288.5 25.1 %all_to_all.88 = bf16[16,16,2560]{2,1,0:T(8,128)(2,1)S(1)} all-to-all(bf16[16,16,2560]{2,1,0:T(8,128)(2,1)S(1)} %temporal.4), channel_id=1, replica_groups=mesh['z'=4,'c'=2,'yh'=2,'yl'=2,'x'=4] {'z','c','yh'}, dimensions={0} | all-to-all | bytes 2621440 | tf_op jit(solution)/shard_map/cond/branch_0_fun/all_to_all | solution.py:307
  313.6 2.7 unpack.4
  (21 shorter events, 9.9 us)
Async XLA Ops:
  7.1 1.3 copy-start.4
  8.4 6.9 %copy-start.26 = (s32[32]{0:T(128)S(1)}, s32[32]{0:T(128)}, u32[]{:S(2)}) copy-start(s32[32]{0:T(128)} %get-tuple-element.40.kind_ref) | copy-start | bytes 388 | tf_op jit(solution)/shard_map/cond
  8.4 37.4 %all-to-all-start = ((bf16[16,256,256]{2,1,0:T(8,128)(2,1)}), bf16[16,256,256]{2,1,0:T(8,128)(2,1)S(1)}, u32[]{:S(2)}, u32[]{:S(2)}) async-start(bf16[16,256,256]{2,1,0:T(8,128)(2,1)} %copy-done.4), calls=%async_computation | async-start | bytes 4194304 | tf_op jit(solution)/shard_map/cond/branch_0_fun/all_to_all | solution.py:307
  19.7 1.9 copy-start.12
  21.6 1.0 copy-start.19
  46.8 9.4 %collective-permute-start = (bf16[8,256,256]{2,1,0:T(8,128)(2,1)}, bf16[8,256,256]{2,1,0:T(8,128)(2,1)}, u32[]{:S(2)}, u32[]{:S(2)}) collective-permute-start(bf16[8,256,256]{2,1,0:T(8,128)(2,1)} %slice.30), channel_id=1, source_target_pairs={{0,32},{8,40},{1,33},{9,41},{2,34},{10,42},{3,35},{11,43},{4,36},{... | collective-permute-start | bytes 3145736 | tf_op jit(solution)/shard_map/cond/branch_0_fun/ppermute | solution.py:315
  48.5 7.7 %collective-permute-start.1 = (bf16[8,256,256]{2,1,0:T(8,128)(2,1)}, bf16[8,256,256]{2,1,0:T(8,128)(2,1)}, u32[]{:S(2)}, u32[]{:S(2)}) collective-permute-start(bf16[8,256,256]{2,1,0:T(8,128)(2,1)} %slice.30), channel_id=1, source_target_pairs={{0,64},{8,72},{1,65},{9,73},{2,66},{10,74},{3,67},{11,75},{4,68},{... | collective-permute-start | bytes 3145736 | tf_op jit(solution)/shard_map/cond/branch_0_fun/ppermute | solution.py:315
  50.2 6.1 %collective-permute-start.2 = (bf16[8,256,256]{2,1,0:T(8,128)(2,1)}, bf16[8,256,256]{2,1,0:T(8,128)(2,1)}, u32[]{:S(2)}, u32[]{:S(2)}) collective-permute-start(bf16[8,256,256]{2,1,0:T(8,128)(2,1)} %slice.30), channel_id=1, source_target_pairs={{0,96},{8,104},{1,97},{9,105},{2,98},{10,106},{3,99},{11,107},{4,1... | collective-permute-start | bytes 3145736 | tf_op jit(solution)/shard_map/cond/branch_0_fun/ppermute | solution.py:315
  51.9 20.2 %all-to-all-start.1 = ((bf16[16,256,128]{2,1,0:T(8,128)(2,1)}), bf16[16,256,128]{2,1,0:T(8,128)(2,1)S(1)}, u32[]{:S(2)}, u32[]{:S(2)}) async-start(bf16[16,256,128]{2,1,0:T(8,128)(2,1)} %copy-done.19), calls=%async_computation.1 | async-start | bytes 2097152 | tf_op jit(solution)/shard_map/cond/branch_0_fun/all_to_all | solution.py:307
  72.1 194.6 %all-to-all-start.3 = ((bf16[16,16,7680]{2,1,0:T(8,128)(2,1)}), bf16[16,16,7680]{2,1,0:T(8,128)(2,1)}, u32[]{:S(2)}, u32[]{:S(2)}) async-start(bf16[16,16,7680]{2,1,0:T(8,128)(2,1)} %bitcast.21), calls=%async_computation.3 | async-start | bytes 7864320 | tf_op jit(solution)/shard_map/cond/branch_0_fun/all_to_all | solution.py:307
  85.3 4.1 %collective-permute-start.4 = (bf16[8,256,128]{2,1,0:T(8,128)(2,1)}, bf16[8,256,128]{2,1,0:T(8,128)(2,1)}, u32[]{:S(2)}, u32[]{:S(2)}) collective-permute-start(bf16[8,256,128]{2,1,0:T(8,128)(2,1)} %slice.32), channel_id=1, source_target_pairs={{0,16},{8,24},{32,48},{40,56},{64,80},{72,88},{96,112},{104,120},{... | collective-permute-start | bytes 1572872 | tf_op jit(solution)/shard_map/cond/branch_0_fun/ppermute | solution.py:315
  91.9 4.1 %collective-permute-start.3 = (bf16[8,256,128]{2,1,0:T(8,128)(2,1)}, bf16[8,256,128]{2,1,0:T(8,128)(2,1)}, u32[]{:S(2)}, u32[]{:S(2)}) collective-permute-start(bf16[8,256,128]{2,1,0:T(8,128)(2,1)} %get-tuple-element.117), channel_id=1, source_target_pairs={{0,16},{8,24},{32,48},{40,56},{64,80},{72,88},{96,112},{104,120},{... | collective-permute-start | bytes 1572872 | tf_op jit(solution)/shard_map/cond/branch_0_fun/ppermute | solution.py:315
  97.2 1.0 copy-start.16
  265.8 1.0 copy-start.10
  266.7 21.8 %all-to-all-start.2 = ((bf16[16,256,128]{2,1,0:T(8,128)(2,1)}), bf16[16,256,128]{2,1,0:T(8,128)(2,1)S(1)}, u32[]{:S(2)}, u32[]{:S(2)}) async-start(bf16[16,256,128]{2,1,0:T(8,128)(2,1)} %copy-done.10), calls=%async_computation.2 | async-start | bytes 2097152 | tf_op jit(solution)/shard_map/cond/branch_0_fun/all_to_all | solution.py:307
where the time goes:
time: 322 us; the launch traced here: 317 us
  Pallas kernels  184 us (57%)
  waiting for transfers between devices  51.4 us (16%)
  starting transfers between devices  35.5 us (11%)
  blocking collectives  25.1 us (8%)
  local copies, waits for them, and re-layouts  9.13 us (3%)
  other arithmetic  8.09 us (3%)
    pallas_call x1, Pallas kernels, spatial_attention(): pl.pallas_call(spatial_kernel, grid_spec=grid_spec, out_shape=jax.ShapeDt...  167 us
    all_to_all x4, waiting for transfers between devices, exchange(): return lax.all_to_all(x, group, split_axis=0, concat_axis=0, tiled=True)  47.1 us
    all_to_all x4, starting transfers between devices, exchange(): return lax.all_to_all(x, group, split_axis=0, concat_axis=0, tiled=True)  27.9 us
    all_to_all x1, blocking collectives, exchange(): return lax.all_to_all(x, group, split_axis=0, concat_axis=0, tiled=True)  25.1 us
    ppermute x5, starting transfers between devices, send(): return lax.ppermute(x, SPOT_GROUP, [(spot(*a), spot(*b)) for a, b in pairs])  7.6 us
    pallas_call x2, Pallas kernels, pack(): pl.pallas_call(functools.partial(pack_kernel, plan, len(shapes)), out_sha...  7.56 us
  transfers between devices with their start and end apart: 9, of which 5 were waited for; matrix products, arithmetic and copies ran while one was open for 3% of the time, Pallas kernels for 56%

commit v1 on v0

--- a/solution.py
+++ b/solution.py
@@ -21,7 +21,7 @@
 SPOT_GROUP = ("z", "c", "yh")
 VMEM = 48 * 1024 * 1024
 
-CASES = ((1, 0, 20), (1, 1, 16), (1, 0, 32), (2, 0, 8))
+CASES = ((1, 0, 20), (1, 1, 16), (2, 0, 32))
 
 
 def order_heads(kind_ref, order_ref):
@@ -236,7 +236,7 @@
             pl.BlockSpec(whole, lambda j, u, g, first: (u, 0, keys_at + j)),
             pl.BlockSpec(whole, lambda j, u, g, first: (u, 0, keys_at + width + j)),
             pl.BlockSpec(whole, lambda j, u, g, first: (0, 0, j)),
-            pl.BlockSpec(whole, lambda j, u, g, first: (0, 0, j)),
+            pl.BlockSpec(whole, lambda j, u, g, first: (0, 0, width + j)),
         ],
         out_specs=pl.BlockSpec(part, lambda j, u, g, first: (u * steps + g, 0, j)),
         scratch_shapes=[
@@ -258,7 +258,7 @@
             transcendentals=units * 2**16,
         ),
         name="spatial",
-    )(first, q, kv, kv, *kv0)
+    )(first, q, kv, kv, kv0, kv0)
 
 
 SPOTS = ROWS // FRAMES
@@ -328,9 +328,80 @@
 
 def to_core(ring):
     pairs = [((i, 0, h), (i, 1, h)) for i in range(4) for h in range(2)]
-    cols = ring.shape[2] // 2
-    own = lax.axis_index("c") == 0
-    return [jnp.where(own, x, send(x, pairs)) for x in (ring[:, :, :cols], ring[:, :, cols:])]
+    return jnp.where(lax.axis_index("c") == 0, ring, send(ring, pairs))
+
+
+def along(x, axis, step):
+    return lax.ppermute(x, axis, [(i, (i + step) % 4) for i in range(4)])
+
+
+Y_AXIS = ("yh", "yl")
+
+
+def place_x():
+    return lax.axis_index("x")
+
+
+def place_y():
+    return lax.axis_index("yh") * 2 + lax.axis_index("yl")
+
+
+def run_copies(copies):
+    for copy in copies:
+        copy.start()
+    for copy in copies:
+        copy.wait()
+
+
+def shuffle(kernel, outs, n_copies, name, *args):
+    return pl.pallas_call(
+        kernel,
+        out_shape=tuple(jax.ShapeDtypeStruct(shape, jnp.bfloat16) for shape in outs),
+        in_specs=[pl.BlockSpec(memory_space=pl.ANY)] * len(args),
+        out_specs=(pl.BlockSpec(memory_space=pltpu.VMEM),) * len(outs),
+        scratch_shapes=[pltpu.SemaphoreType.DMA((n_copies,))],
+        compiler_params=pltpu.CompilerParams(vmem_limit_bytes=VMEM),
+        name=name,
+    )(*args)
+
+
+def pick_kernel(ref, *refs):
+    outs, sems = refs[:4], refs[4]
+    y = place_y()
+    run_copies(
+        [
+            pltpu.make_async_copy(ref.at[pl.ds((y + step) % 4 * 4, 4)], out, sems.at[step])
+            for step, out in enumerate(outs)
+        ]
+    )
+
+
+def turn_kernel(*refs):
+    ins, outs, sems = refs[:4], refs[4:8], refs[8]
+    x, y = place_x(), place_y()
+    run_copies(
+        [
+            pltpu.make_async_copy(
+                ref.at[(x + step) % 4], out.at[(y + 4 - back) % 4], sems.at[4 * step + back]
+            )
+            for step, out in enumerate(outs)
+            for back, ref in enumerate(ins)
+        ]
+    )
+
+
+def settle_kernel(*refs):
+    ins, out, sems = refs[:4], refs[4], refs[5]
+    x = place_x()
+    run_copies(
+        [
+            pltpu.make_async_copy(
+                ref.at[y], out.at[4 * y + (x + 4 - back) % 4], sems.at[4 * back + y]
+            )
+            for back, ref in enumerate(ins)
+            for y in range(4)
+        ]
+    )
 
 
 def attend(a, b, ct, queries, keys, values, head_kind):
@@ -351,39 +422,52 @@
 
     plan = [(0, part, a, 0, wide, name) for part, name in enumerate("kv")]
     (kv_send,) = pack(plan, [(wide, ROWS, 2 * a * HEAD_DIM)], *arrays)
-    if b:
-        qkv_b, kv_send = lax.optimization_barrier((qkv_b, kv_send))
-    kv_a = exchange(kv_send, BLOCK_GROUP)
-    if b:
-        ring_b = along_y(along_z(qkv_b[:, :, b * HEAD_DIM :], (0,)))
-
     plan = [(0, 0, a, 0, wide, "q")]
     plan += [(1, part, ct, None, 1, name) for part, name in enumerate("qkv")]
     shapes = [(wide, ROWS, a * HEAD_DIM), (1, ROWS, 3 * ct * HEAD_DIM)]
     q_send, t_send = pack(plan, shapes, *arrays)
+    if b:
+        qkv_b, kv_send, q_send, t_send = lax.optimization_barrier((qkv_b, kv_send, q_send, t_send))
+    kv_a = exchange(kv_send, BLOCK_GROUP)
+    if b:
+        zero_b = to_core(along_y(along_z(qkv_b[:, :, b * HEAD_DIM :], (0,))))
+
     kv_a, q_send = lax.optimization_barrier((kv_a, q_send))
     q_a = exchange(q_send, BLOCK_GROUP)
     ring_a = along_z(kv_a[:RANKS], (0, 1))
 
     t_send = t_send.reshape(FRAMES, SPOTS, 3 * ct * HEAD_DIM)
     if b:
-        q_a, ring_a, ring_b, t_send = lax.optimization_barrier((q_a, ring_a, ring_b, t_send))
+        q_a, ring_a, zero_b, t_send = lax.optimization_barrier((q_a, ring_a, zero_b, t_send))
     else:
         q_a, ring_a, t_send = lax.optimization_barrier((q_a, ring_a, t_send))
     t_have = exchange(t_send, SPOT_GROUP)
 
-    backs, layouts = [], []
+    at = unit(z + c == 0, 0, BLOCK_GROUP, wide, a)
+    layouts = [(a, 0, wide)]
     if b:
-        at = unit(z + c + yh == 0, a * wide, FRAME_GROUP, narrow, b)
-        out = spatial_attention(b, 1, at, qkv_b, qkv_b, b, to_core(ring_b))
-        out, t_have = lax.optimization_barrier((out, t_have))
-        backs.append(exchange(out, FRAME_GROUP))
+        at_b = unit(z + c + yh == 0, a * wide, FRAME_GROUP, narrow, b)
+        out_b = spatial_attention(b, 1, at_b, qkv_b, qkv_b, b, zero_b)
+        q_a, out_b = lax.optimization_barrier((q_a, out_b))
+        out = spatial_attention(a, 2, at, q_a, kv_a, 0, to_core(ring_a))
+        out_b, out, t_have = lax.optimization_barrier((out_b, out, t_have))
+        back_b = exchange(out_b, FRAME_GROUP)
+        out, back_b = lax.optimization_barrier((out, back_b))
         layouts.append((b, a * wide, narrow))
-    at = unit(z + c == 0, 0, BLOCK_GROUP, wide, a)
-    out = spatial_attention(a, 2, at, q_a, kv_a, 0, to_core(ring_a))
-    backs.append(exchange(out, BLOCK_GROUP))
-    layouts.append((a, 0, wide))
-    t_out = temporal_attention(ct, t_have)
+        backs = [exchange(out, BLOCK_GROUP), back_b]
+        t_out = temporal_attention(ct, t_have)
+    else:
+        out = spatial_attention(a, 2, at, q_a, kv_a, 0, to_core(ring_a))
+        part = [(4, ROWS, a * HEAD_DIM)] * 4
+        to_y = shuffle(pick_kernel, part, 4, "pick", out)
+        on_y = [to_y[0]] + [along(to_y[step], Y_AXIS, step) for step in (1, 2, 3)]
+        t_have = lax.optimization_barrier((t_have, to_y))[0]
+        t_out = temporal_attention(ct, t_have)
+        on_y, t_out = lax.optimization_barrier((on_y, t_out))
+        to_x = shuffle(turn_kernel, part, 16, "turn", *on_y)
+        t_out, to_x = lax.optimization_barrier((t_out, to_x))
+        on_x = [to_x[0]] + [along(to_x[step], "x", step) for step in (1, 2, 3)]
+        backs = shuffle(settle_kernel, [(16, ROWS, a * HEAD_DIM)], 16, "settle", *on_x)
     t_back = exchange(t_out, SPOT_GROUP).reshape(ROWS, ct * HEAD_DIM)
     return unpack(layouts, ct, head_kind, backs, t_back)
 

time: 322 us -> 305 us (0.947)
  blocking collectives: 25.1 us -> 0 us
  starting transfers between devices: 35.5 us -> 43.2 us
  waiting for transfers between devices: 51.4 us -> 56.9 us
  local copies, waits for them, and re-layouts: 9.13 us -> 5.26 us
    all_to_all x1 -> x0, blocking collectives: 25.1 us -> none  [exchange(): return lax.all_to_all(x, group, split_axis=0, concat_axis=0, tiled=True)]
    ppermute x0 -> x6, waiting for transfers between devices: none -> 16.6 us  [along(): return lax.ppermute(x, axis, [(i, (i + step) % 4) for i in range(4)])]
    all_to_all x4, waiting for transfers between devices: 47.1 us -> 38.2 us  [exchange(): return lax.all_to_all(x, group, split_axis=0, concat_axis=0, tiled=True)]
    ppermute x0 -> x6, starting transfers between devices: none -> 7.88 us  [along(): return lax.ppermute(x, axis, [(i, (i + step) % 4) for i in range(4)])]
    ppermute x5 -> x4, starting transfers between devices: 7.6 us -> 6.3 us  [send(): return lax.ppermute(x, SPOT_GROUP, [(spot(*a), spot(*b)) for a, b in pairs])]
  transfers between devices with their start and end apart: 9 -> 14, of which waited for: 5 -> 8; matrix products, arithmetic and copies ran while one was open for 3% -> 1% of each run, Pallas kernels for 56% -> 60%
where the time goes in v1:
time: 305 us; the launch traced here: 302 us
  Pallas kernels  187 us (61%)
  waiting for transfers between devices  56.9 us (19%)
  starting transfers between devices  43.2 us (14%)
  other arithmetic  5.81 us (2%)
  local copies, waits for them, and re-layouts  5.26 us (2%)
    pallas_call x1, Pallas kernels, spatial_attention(): pl.pallas_call(spatial_kernel, grid_spec=grid_spec, out_shape=jax.ShapeDt...  167 us
    all_to_all x4, waiting for transfers between devices, exchange(): return lax.all_to_all(x, group, split_axis=0, concat_axis=0, tiled=True)  38.2 us
    all_to_all x4, starting transfers between devices, exchange(): return lax.all_to_all(x, group, split_axis=0, concat_axis=0, tiled=True)  29 us
    ppermute x6, waiting for transfers between devices, along(): return lax.ppermute(x, axis, [(i, (i + step) % 4) for i in range(4)])  16.6 us
    ppermute x6, starting transfers between devices, along(): return lax.ppermute(x, axis, [(i, (i + step) % 4) for i in range(4)])  7.88 us
    pallas_call x2, Pallas kernels, pack(): pl.pallas_call(functools.partial(pack_kernel, plan, len(shapes)), out_sha...  7.56 us
    pallas_call x1, Pallas kernels, temporal_attention(): pl.pallas_call(temporal_kernel, grid=(steps,), in_specs=[pl.BlockSpec(blo...  6.76 us
    ppermute x4, starting transfers between devices, send(): return lax.ppermute(x, SPOT_GROUP, [(spot(*a), spot(*b)) for a, b in pairs])  6.3 us
  transfers between devices with their start and end apart: 14, of which 8 were waited for; matrix products, arithmetic and copies ran while one was open for 1% of the time, Pallas kernels for 60%

profile of v1, /device:TPU:97, one launch (start us, length us, event | category | flops | bytes accessed | tf_op | source)
XLA Modules:
  0.0 301.6 jit_solution(518112838696736976)
XLA Ops:
  3.3 298.2 %conditional.1 = (bf16[256,4096]{1,0:T(8,128)(2,1)}) conditional(s32[]{:T(128)} %clamp.3, (s32[32]{0:T(128)}, bf16[256,4096]{1,0:T(8,128)(2,1)}, bf16[256,4096]{1,0:T(8,128)(2,1)}, bf16[256,4096]{1,0:T(8,128)(2,1)}) %tuple.30, (s32[32]{0:T(128)}, bf16[256,4096]{1,0:T(8,128)(2,1)}, bf16[256,4096]{1,0:T(8,128)(2,1)}, ...), branch_computations={%region_1.3_spmd, %region_3.5_spmd, %region_5.7_spmd} | conditional | flops 1346371584 | bytes 186845600 | solution.py:484
  3.3 3.2 %pack.7 = bf16[16,256,256]{2,1,0:T(8,128)(2,1)S(1)} custom-call(s32[32]{0:T(128)} %get-tuple-element.32.kind_ref, bf16[256,4096]{1,0:T(8,128)(2,1)} %get-tuple-element.126.q_ref, bf16[256,4096]{1,0:T(8,128)(2,1)} %get-tuple-element.129.k_ref, bf16[256,4096]{1,0:T(8,128)(2,1)} %get-tuple-element.132.v_ref), custom_call_target="tpu_custom_call" | custom-call | tf_op jit(solution)/shard_map/cond/branch_0_fun/pack/pallas_call | solution.py:82
  7.8 6.9 %all-to-all-start = ((bf16[16,256,256]{2,1,0:T(8,128)(2,1)}), bf16[16,256,256]{2,1,0:T(8,128)(2,1)S(1)}, u32[]{:S(2)}, u32[]{:S(2)}) async-start(bf16[16,256,256]{2,1,0:T(8,128)(2,1)} %copy-done.7), calls=%async_computation | async-start | bytes 4194304 | tf_op jit(solution)/shard_map/cond/branch_0_fun/all_to_all | solution.py:307
  14.7 4.4 %pack.8 = (bf16[16,256,128]{2,1,0:T(8,128)(2,1)S(1)}, bf16[1,256,7680]{2,1,0:T(8,128)(2,1)S(1)}) custom-call(s32[32]{0:T(128)S(1)} %copy-done.25, bf16[256,4096]{1,0:T(8,128)(2,1)} %get-tuple-element.126.q_ref, bf16[256,4096]{1,0:T(8,128)(2,1)} %get-tuple-element.129.k_ref, bf16[256,4096]{1,0:T(8,128)(2,1)} %get-tuple-element.132.v_ref), custom_call_target="tpu_custom_call" | custom-call | tf_op jit(solution)/shard_map/cond/branch_0_fun/pack/pallas_call | solution.py:82
  19.1 1.9 copy-done.13
  22.0 23.2 %all-to-all-done.refs_1_.refs_2_ = bf16[16,256,256]{2,1,0:T(8,128)(2,1)S(1)} async-done(((bf16[16,256,256]{2,1,0:T(8,128)(2,1)}), bf16[16,256,256]{2,1,0:T(8,128)(2,1)S(1)}, u32[]{:S(2)}, u32[]{:S(2)}) %all-to-all-start) | async-done | bytes 2097184 | tf_op jit(solution)/shard_map/cond/branch_0_fun/all_to_all | solution.py:307
  46.2 1.7 collective-permute-start
  47.8 1.6 collective-permute-start.1
  49.5 1.7 collective-permute-start.2
  51.2 4.3 %all-to-all-start.1 = ((bf16[16,256,128]{2,1,0:T(8,128)(2,1)}), bf16[16,256,128]{2,1,0:T(8,128)(2,1)S(1)}, u32[]{:S(2)}, u32[]{:S(2)}) async-start(bf16[16,256,128]{2,1,0:T(8,128)(2,1)} %copy-done.17), calls=%async_computation.1 | async-start | bytes 2097152 | tf_op jit(solution)/shard_map/cond/branch_0_fun/all_to_all | solution.py:307
  55.5 2.4 select_select_fusion
  57.9 13.5 %all-to-all-done.1.refs_0_ = bf16[16,256,128]{2,1,0:T(8,128)(2,1)S(1)} async-done(((bf16[16,256,128]{2,1,0:T(8,128)(2,1)}), bf16[16,256,128]{2,1,0:T(8,128)(2,1)S(1)}, u32[]{:S(2)}, u32[]{:S(2)}) %all-to-all-start.1) | async-done | bytes 1048608 | tf_op jit(solution)/shard_map/cond/branch_0_fun/all_to_all | solution.py:307
  71.4 11.4 %all-to-all-start.2 = ((bf16[16,16,7680]{2,1,0:T(8,128)(2,1)}), bf16[16,16,7680]{2,1,0:T(8,128)(2,1)}, u32[]{:S(2)}, u32[]{:S(2)}) async-start(bf16[16,16,7680]{2,1,0:T(8,128)(2,1)} %bitcast.17), calls=%async_computation.2 | async-start | bytes 7864320 | tf_op jit(solution)/shard_map/cond/branch_0_fun/all_to_all | solution.py:307
  85.6 2.1 collective-permute-done.3
  89.0 167.1 %spatial.4.ref = bf16[16,256,128]{2,1,0:T(8,128)(2,1)S(1)} custom-call(s32[2]{0:T(128)S(1)} %pad_add_fusion.first_ref, bf16[16,256,128]{2,1,0:T(8,128)(2,1)S(1)} %all-to-all-done.1.refs_0_, bf16[16,256,256]{2,1,0:T(8,128)(2,1)S(1)} %all-to-all-done.refs_1_.refs_2_, bf16[16,256,256]{2,1,0:T(8,128)(2,1)S(1)} %all-to-all-done.refs_1_.refs_2_, ...), custom_call_target="tpu_custom_call" | custom-call | flops 134217728 | bytes 131072 | tf_op jit(solution)/shard_map/cond/branch_0_fun/spatial/pallas_call | solution.py:250
  257.6 3.3 %collective-permute-start.5 = (bf16[4,256,128]{2,1,0:T(8,128)(2,1)S(1)}, bf16[4,256,128]{2,1,0:T(8,128)(2,1)S(1)}, u32[]{:S(2)}, u32[]{:S(2)}) collective-permute-start(bf16[4,256,128]{2,1,0:T(8,128)(2,1)S(1)} %get-tuple-element.45), channel_id=1, source_target_pairs={{0,8},{4,12},{8,0},{12,4},{1,9},{5,13},{9,1},{13,5},{2,10},{6,14},... | collective-permute-start | bytes 786440 | tf_op jit(solution)/shard_map/cond/branch_0_fun/ppermute | solution.py:335
  261.0 6.8 %temporal.3 = bf16[16,16,2560]{2,1,0:T(8,128)(2,1)} custom-call(bf16[16,16,7680]{2,1,0:T(8,128)(2,1)} %all-to-all-done.2.q_ref.k_ref.v_ref, bf16[16,16,7680]{2,1,0:T(8,128)(2,1)} %all-to-all-done.2.q_ref.k_ref.v_ref, bf16[16,16,7680]{2,1,0:T(8,128)(2,1)} %all-to-all-done.2.q_ref.k_ref.v_ref), custom_call_target="tpu_custom_call" | custom-call | flops 671088640 | bytes 5242880 | tf_op jit(solution)/shard_map/cond/branch_0_fun/temporal/pallas_call | solution.py:286
  267.8 5.0 %collective-permute-done.5.refs_2_ = bf16[4,256,128]{2,1,0:T(8,128)(2,1)S(1)} collective-permute-done((bf16[4,256,128]{2,1,0:T(8,128)(2,1)S(1)}, bf16[4,256,128]{2,1,0:T(8,128)(2,1)S(1)}, u32[]{:S(2)}, u32[]{:S(2)}) %collective-permute-start.5) | collective-permute-done | bytes 262176 | tf_op jit(solution)/shard_map/cond/branch_0_fun/ppermute | solution.py:335
  274.3 6.5 %all-to-all-start.3 = ((bf16[16,16,2560]{2,1,0:T(8,128)(2,1)}), bf16[16,16,2560]{2,1,0:T(8,128)(2,1)S(1)}, u32[]{:S(2)}, u32[]{:S(2)}) async-start(bf16[16,16,2560]{2,1,0:T(8,128)(2,1)} %temporal.3), calls=%async_computation.3 | async-start | bytes 2621440 | tf_op jit(solution)/shard_map/cond/branch_0_fun/all_to_all | solution.py:307
  280.8 2.8 collective-permute-start.8
  283.9 5.7 %collective-permute-done.7.refs_1_ = bf16[4,256,128]{2,1,0:T(8,128)(2,1)S(1)} collective-permute-done((bf16[4,256,128]{2,1,0:T(8,128)(2,1)S(1)}, bf16[4,256,128]{2,1,0:T(8,128)(2,1)S(1)}, u32[]{:S(2)}, u32[]{:S(2)}) %collective-permute-start.7) | collective-permute-done | bytes 262176 | tf_op jit(solution)/shard_map/cond/branch_0_fun/ppermute | solution.py:335
  289.6 5.7 %collective-permute-done.8.refs_2_ = bf16[4,256,128]{2,1,0:T(8,128)(2,1)S(1)} collective-permute-done((bf16[4,256,128]{2,1,0:T(8,128)(2,1)S(1)}, bf16[4,256,128]{2,1,0:T(8,128)(2,1)S(1)}, u32[]{:S(2)}, u32[]{:S(2)}) %collective-permute-start.8) | collective-permute-done | bytes 262176 | tf_op jit(solution)/shard_map/cond/branch_0_fun/ppermute | solution.py:335
  297.0 1.5 all-to-all-done.3
  298.5 2.7 unpack.3
  (27 shorter events, 13.2 us)
Async XLA Ops:
  6.4 1.3 copy-start.7
  7.8 6.9 %copy-start.25 = (s32[32]{0:T(128)S(1)}, s32[32]{0:T(128)}, u32[]{:S(2)}) copy-start(s32[32]{0:T(128)} %get-tuple-element.32.kind_ref) | copy-start | bytes 388 | tf_op jit(solution)/shard_map/cond
  7.8 37.4 %all-to-all-start = ((bf16[16,256,256]{2,1,0:T(8,128)(2,1)}), bf16[16,256,256]{2,1,0:T(8,128)(2,1)S(1)}, u32[]{:S(2)}, u32[]{:S(2)}) async-start(bf16[16,256,256]{2,1,0:T(8,128)(2,1)} %copy-done.7), calls=%async_computation | async-start | bytes 4194304 | tf_op jit(solution)/shard_map/cond/branch_0_fun/all_to_all | solution.py:307
  19.1 1.9 copy-start.13
  21.0 1.0 copy-start.17
  46.2 9.3 %collective-permute-start = (bf16[8,256,256]{2,1,0:T(8,128)(2,1)}, bf16[8,256,256]{2,1,0:T(8,128)(2,1)}, u32[]{:S(2)}, u32[]{:S(2)}) collective-permute-start(bf16[8,256,256]{2,1,0:T(8,128)(2,1)} %slice.8), channel_id=1, source_target_pairs={{0,32},{8,40},{1,33},{9,41},{2,34},{10,42},{3,35},{11,43},{4,36},{... | collective-permute-start | bytes 3145736 | tf_op jit(solution)/shard_map/cond/branch_0_fun/ppermute | solution.py:315
  47.8 7.7 %collective-permute-start.1 = (bf16[8,256,256]{2,1,0:T(8,128)(2,1)}, bf16[8,256,256]{2,1,0:T(8,128)(2,1)}, u32[]{:S(2)}, u32[]{:S(2)}) collective-permute-start(bf16[8,256,256]{2,1,0:T(8,128)(2,1)} %slice.8), channel_id=1, source_target_pairs={{0,64},{8,72},{1,65},{9,73},{2,66},{10,74},{3,67},{11,75},{4,68},{... | collective-permute-start | bytes 3145736 | tf_op jit(solution)/shard_map/cond/branch_0_fun/ppermute | solution.py:315
  49.5 6.0 %collective-permute-start.2 = (bf16[8,256,256]{2,1,0:T(8,128)(2,1)}, bf16[8,256,256]{2,1,0:T(8,128)(2,1)}, u32[]{:S(2)}, u32[]{:S(2)}) collective-permute-start(bf16[8,256,256]{2,1,0:T(8,128)(2,1)} %slice.8), channel_id=1, source_target_pairs={{0,96},{8,104},{1,97},{9,105},{2,98},{10,106},{3,99},{11,107},{4,1... | collective-permute-start | bytes 3145736 | tf_op jit(solution)/shard_map/cond/branch_0_fun/ppermute | solution.py:315
  51.2 20.2 %all-to-all-start.1 = ((bf16[16,256,128]{2,1,0:T(8,128)(2,1)}), bf16[16,256,128]{2,1,0:T(8,128)(2,1)S(1)}, u32[]{:S(2)}, u32[]{:S(2)}) async-start(bf16[16,256,128]{2,1,0:T(8,128)(2,1)} %copy-done.17), calls=%async_computation.1 | async-start | bytes 2097152 | tf_op jit(solution)/shard_map/cond/branch_0_fun/all_to_all | solution.py:307
  71.4 189.6 %all-to-all-start.2 = ((bf16[16,16,7680]{2,1,0:T(8,128)(2,1)}), bf16[16,16,7680]{2,1,0:T(8,128)(2,1)}, u32[]{:S(2)}, u32[]{:S(2)}) async-start(bf16[16,16,7680]{2,1,0:T(8,128)(2,1)} %bitcast.17), calls=%async_computation.2 | async-start | bytes 7864320 | tf_op jit(solution)/shard_map/cond/branch_0_fun/all_to_all | solution.py:307
  82.8 4.9 %collective-permute-start.3 = (bf16[8,256,256]{2,1,0:T(8,128)(2,1)}, bf16[8,256,256]{2,1,0:T(8,128)(2,1)}, u32[]{:S(2)}, u32[]{:S(2)}) collective-permute-start(bf16[8,256,256]{2,1,0:T(8,128)(2,1)} %select_select_fusion), channel_id=1, source_target_pairs={{0,16},{8,24},{32,48},{40,56},{64,80},{72,88},{96,112},{104,120},{... | collective-permute-start | bytes 3145736 | tf_op jit(solution)/shard_map/cond/branch_0_fun/ppermute | solution.py:315
  256.2 11.6 %collective-permute-start.4 = (bf16[4,256,128]{2,1,0:T(8,128)(2,1)S(1)}, bf16[4,256,128]{2,1,0:T(8,128)(2,1)S(1)}, u32[]{:S(2)}, u32[]{:S(2)}) collective-permute-start(bf16[4,256,128]{2,1,0:T(8,128)(2,1)S(1)} %get-tuple-element.44), channel_id=1, source_target_pairs={{0,4},{4,8},{8,12},{12,0},{1,5},{5,9},{9,13},{13,1},{2,6},{6,10},{... | collective-permute-start | bytes 786440 | tf_op jit(solution)/shard_map/cond/branch_0_fun/ppermute | solution.py:335
  257.6 15.2 %collective-permute-start.5 = (bf16[4,256,128]{2,1,0:T(8,128)(2,1)S(1)}, bf16[4,256,128]{2,1,0:T(8,128)(2,1)S(1)}, u32[]{:S(2)}, u32[]{:S(2)}) collective-permute-start(bf16[4,256,128]{2,1,0:T(8,128)(2,1)S(1)} %get-tuple-element.45), channel_id=1, source_target_pairs={{0,8},{4,12},{8,0},{12,4},{1,9},{5,13},{9,1},{13,5},{2,10},{6,14},... | collective-permute-start | bytes 786440 | tf_op jit(solution)/shard_map/cond/branch_0_fun/ppermute | solution.py:335
  260.9 11.9 %collective-permute-start.6 = (bf16[4,256,128]{2,1,0:T(8,128)(2,1)S(1)}, bf16[4,256,128]{2,1,0:T(8,128)(2,1)S(1)}, u32[]{:S(2)}, u32[]{:S(2)}) collective-permute-start(bf16[4,256,128]{2,1,0:T(8,128)(2,1)S(1)} %get-tuple-element.46), channel_id=1, source_target_pairs={{0,12},{4,0},{8,4},{12,8},{1,13},{5,1},{9,5},{13,9},{2,14},{6,2},{... | collective-permute-start | bytes 786440 | tf_op jit(solution)/shard_map/cond/branch_0_fun/ppermute | solution.py:335
  274.3 24.2 %all-to-all-start.3 = ((bf16[16,16,2560]{2,1,0:T(8,128)(2,1)}), bf16[16,16,2560]{2,1,0:T(8,128)(2,1)S(1)}, u32[]{:S(2)}, u32[]{:S(2)}) async-start(bf16[16,16,2560]{2,1,0:T(8,128)(2,1)} %temporal.3), calls=%async_computation.3 | async-start | bytes 2621440 | tf_op jit(solution)/shard_map/cond/branch_0_fun/all_to_all | solution.py:307
  280.8 8.7 %collective-permute-start.7 = (bf16[4,256,128]{2,1,0:T(8,128)(2,1)S(1)}, bf16[4,256,128]{2,1,0:T(8,128)(2,1)S(1)}, u32[]{:S(2)}, u32[]{:S(2)}) collective-permute-start(bf16[4,256,128]{2,1,0:T(8,128)(2,1)S(1)} %get-tuple-element.59), channel_id=1, source_target_pairs={{0,1},{1,2},{2,3},{3,0},{4,5},{5,6},{6,7},{7,4},{8,9},{9,10},{10,1... | collective-permute-start | bytes 786440 | tf_op jit(solution)/shard_map/cond/branch_0_fun/ppermute | solution.py:335
  280.8 14.5 %collective-permute-start.8 = (bf16[4,256,128]{2,1,0:T(8,128)(2,1)S(1)}, bf16[4,256,128]{2,1,0:T(8,128)(2,1)S(1)}, u32[]{:S(2)}, u32[]{:S(2)}) collective-permute-start(bf16[4,256,128]{2,1,0:T(8,128)(2,1)S(1)} %get-tuple-element.60), channel_id=1, source_target_pairs={{0,2},{1,3},{2,0},{3,1},{4,6},{5,7},{6,4},{7,5},{8,10},{9,11},{10,... | collective-permute-start | bytes 786440 | tf_op jit(solution)/shard_map/cond/branch_0_fun/ppermute | solution.py:335
  283.6 11.9 %collective-permute-start.9 = (bf16[4,256,128]{2,1,0:T(8,128)(2,1)S(1)}, bf16[4,256,128]{2,1,0:T(8,128)(2,1)S(1)}, u32[]{:S(2)}, u32[]{:S(2)}) collective-permute-start(bf16[4,256,128]{2,1,0:T(8,128)(2,1)S(1)} %get-tuple-element.61), channel_id=1, source_target_pairs={{0,3},{1,0},{2,1},{3,2},{4,7},{5,4},{6,5},{7,6},{8,11},{9,8},{10,9... | collective-permute-start | bytes 786440 | tf_op jit(solution)/shard_map/cond/branch_0_fun/ppermute | solution.py:335

commit v2 on v1

--- a/solution.py
+++ b/solution.py
@@ -449,25 +449,25 @@
         at_b = unit(z + c + yh == 0, a * wide, FRAME_GROUP, narrow, b)
         out_b = spatial_attention(b, 1, at_b, qkv_b, qkv_b, b, zero_b)
         q_a, out_b = lax.optimization_barrier((q_a, out_b))
-        out = spatial_attention(a, 2, at, q_a, kv_a, 0, to_core(ring_a))
-        out_b, out, t_have = lax.optimization_barrier((out_b, out, t_have))
+        layouts.append((b, a * wide, narrow))
+    out = spatial_attention(a, 2, at, q_a, kv_a, 0, to_core(ring_a))
+
+    part = [(4, ROWS, a * HEAD_DIM)] * 4
+    to_y = shuffle(pick_kernel, part, 4, "pick", out)
+    on_y = [to_y[0]] + [along(to_y[step], Y_AXIS, step) for step in (1, 2, 3)]
+    t_have = lax.optimization_barrier((t_have, to_y, out_b if b else to_y))[0]
+    t_out = temporal_attention(ct, t_have)
+    backs = []
+    if b:
+        out_b, _ = lax.optimization_barrier((out_b, t_have))
         back_b = exchange(out_b, FRAME_GROUP)
-        out, back_b = lax.optimization_barrier((out, back_b))
-        layouts.append((b, a * wide, narrow))
-        backs = [exchange(out, BLOCK_GROUP), back_b]
-        t_out = temporal_attention(ct, t_have)
-    else:
-        out = spatial_attention(a, 2, at, q_a, kv_a, 0, to_core(ring_a))
-        part = [(4, ROWS, a * HEAD_DIM)] * 4
-        to_y = shuffle(pick_kernel, part, 4, "pick", out)
-        on_y = [to_y[0]] + [along(to_y[step], Y_AXIS, step) for step in (1, 2, 3)]
-        t_have = lax.optimization_barrier((t_have, to_y))[0]
-        t_out = temporal_attention(ct, t_have)
-        on_y, t_out = lax.optimization_barrier((on_y, t_out))
-        to_x = shuffle(turn_kernel, part, 16, "turn", *on_y)
-        t_out, to_x = lax.optimization_barrier((t_out, to_x))
-        on_x = [to_x[0]] + [along(to_x[step], "x", step) for step in (1, 2, 3)]
-        backs = shuffle(settle_kernel, [(16, ROWS, a * HEAD_DIM)], 16, "settle", *on_x)
+        t_out, back_b = lax.optimization_barrier((t_out, back_b))
+        backs.append(back_b)
+    on_y, t_out = lax.optimization_barrier((on_y, t_out))
+    to_x = shuffle(turn_kernel, part, 16, "turn", *on_y)
+    t_out, to_x = lax.optimization_barrier((t_out, to_x))
+    on_x = [to_x[0]] + [along(to_x[step], "x", step) for step in (1, 2, 3)]
+    backs = list(shuffle(settle_kernel, [(16, ROWS, a * HEAD_DIM)], 16, "settle", *on_x)) + backs
     t_back = exchange(t_out, SPOT_GROUP).reshape(ROWS, ct * HEAD_DIM)
     return unpack(layouts, ct, head_kind, backs, t_back)
 

time: 305 us -> 305 us (level)
  no operation moved by 1% of the time
where the time goes in v2:
time: 305 us; the launch traced here: 302 us
  Pallas kernels  187 us (61%)
  waiting for transfers between devices  57.1 us (19%)
  starting transfers between devices  43.2 us (14%)
  other arithmetic  5.73 us (2%)
  local copies, waits for them, and re-layouts  5.24 us (2%)
    pallas_call x1, Pallas kernels, spatial_attention(): pl.pallas_call(spatial_kernel, grid_spec=grid_spec, out_shape=jax.ShapeDt...  167 us
    all_to_all x4, waiting for transfers between devices, exchange(): return lax.all_to_all(x, group, split_axis=0, concat_axis=0, tiled=True)  38.2 us
    all_to_all x4, starting transfers between devices, exchange(): return lax.all_to_all(x, group, split_axis=0, concat_axis=0, tiled=True)  29 us
    ppermute x6, waiting for transfers between devices, along(): return lax.ppermute(x, axis, [(i, (i + step) % 4) for i in range(4)])  16.6 us
    ppermute x6, starting transfers between devices, along(): return lax.ppermute(x, axis, [(i, (i + step) % 4) for i in range(4)])  7.88 us
    pallas_call x2, Pallas kernels, pack(): pl.pallas_call(functools.partial(pack_kernel, plan, len(shapes)), out_sha...  7.56 us
    pallas_call x1, Pallas kernels, temporal_attention(): pl.pallas_call(temporal_kernel, grid=(steps,), in_specs=[pl.BlockSpec(blo...  6.76 us
    ppermute x4, starting transfers between devices, send(): return lax.ppermute(x, SPOT_GROUP, [(spot(*a), spot(*b)) for a, b in pairs])  6.33 us
  transfers between devices with their start and end apart: 14, of which 8 were waited for; matrix products, arithmetic and copies ran while one was open for 1% of the time, Pallas kernels for 60%

profile of v2, /device:TPU:97, one launch (start us, length us, event | category | flops | bytes accessed | tf_op | source)
XLA Modules:
  0.0 301.6 jit_solution(16974914607401348091)
XLA Ops:
  3.3 298.2 %conditional.1 = (bf16[256,4096]{1,0:T(8,128)(2,1)}) conditional(s32[]{:T(128)} %clamp.3, (s32[32]{0:T(128)}, bf16[256,4096]{1,0:T(8,128)(2,1)}, bf16[256,4096]{1,0:T(8,128)(2,1)}, bf16[256,4096]{1,0:T(8,128)(2,1)}) %tuple.33, (s32[32]{0:T(128)}, bf16[256,4096]{1,0:T(8,128)(2,1)}, bf16[256,4096]{1,0:T(8,128)(2,1)}, ...), branch_computations={%region_1.3_spmd, %region_3.5_spmd, %region_5.7_spmd} | conditional | flops 1346371584 | bytes 185797248 | solution.py:484
  3.3 3.2 %pack.7 = bf16[16,256,256]{2,1,0:T(8,128)(2,1)S(1)} custom-call(s32[32]{0:T(128)} %get-tuple-element.32.kind_ref, bf16[256,4096]{1,0:T(8,128)(2,1)} %get-tuple-element.143.q_ref, bf16[256,4096]{1,0:T(8,128)(2,1)} %get-tuple-element.146.k_ref, bf16[256,4096]{1,0:T(8,128)(2,1)} %get-tuple-element.149.v_ref), custom_call_target="tpu_custom_call" | custom-call | tf_op jit(solution)/shard_map/cond/branch_0_fun/pack/pallas_call | solution.py:82
  7.8 6.9 %all-to-all-start = ((bf16[16,256,256]{2,1,0:T(8,128)(2,1)}), bf16[16,256,256]{2,1,0:T(8,128)(2,1)S(1)}, u32[]{:S(2)}, u32[]{:S(2)}) async-start(bf16[16,256,256]{2,1,0:T(8,128)(2,1)} %copy-done.7), calls=%async_computation | async-start | bytes 4194304 | tf_op jit(solution)/shard_map/cond/branch_0_fun/all_to_all | solution.py:307
  14.7 4.4 %pack.8 = (bf16[16,256,128]{2,1,0:T(8,128)(2,1)S(1)}, bf16[1,256,7680]{2,1,0:T(8,128)(2,1)S(1)}) custom-call(s32[32]{0:T(128)S(1)} %copy-done.26, bf16[256,4096]{1,0:T(8,128)(2,1)} %get-tuple-element.143.q_ref, bf16[256,4096]{1,0:T(8,128)(2,1)} %get-tuple-element.146.k_ref, bf16[256,4096]{1,0:T(8,128)(2,1)} %get-tuple-element.149.v_ref), custom_call_target="tpu_custom_call" | custom-call | tf_op jit(solution)/shard_map/cond/branch_0_fun/pack/pallas_call | solution.py:82
  19.1 1.9 copy-done.11
  22.0 23.2 %all-to-all-done.refs_1_.refs_2_ = bf16[16,256,256]{2,1,0:T(8,128)(2,1)S(1)} async-done(((bf16[16,256,256]{2,1,0:T(8,128)(2,1)}), bf16[16,256,256]{2,1,0:T(8,128)(2,1)S(1)}, u32[]{:S(2)}, u32[]{:S(2)}) %all-to-all-start) | async-done | bytes 2097184 | tf_op jit(solution)/shard_map/cond/branch_0_fun/all_to_all | solution.py:307
  46.2 1.7 collective-permute-start
  47.8 1.7 collective-permute-start.1
  49.5 1.7 collective-permute-start.2
  51.2 4.3 %all-to-all-start.1 = ((bf16[16,256,128]{2,1,0:T(8,128)(2,1)}), bf16[16,256,128]{2,1,0:T(8,128)(2,1)S(1)}, u32[]{:S(2)}, u32[]{:S(2)}) async-start(bf16[16,256,128]{2,1,0:T(8,128)(2,1)} %copy-done.15), calls=%async_computation.1 | async-start | bytes 2097152 | tf_op jit(solution)/shard_map/cond/branch_0_fun/all_to_all | solution.py:307
  55.6 2.4 select_select_fusion
  58.0 13.5 %all-to-all-done.1.refs_0_ = bf16[16,256,128]{2,1,0:T(8,128)(2,1)S(1)} async-done(((bf16[16,256,128]{2,1,0:T(8,128)(2,1)}), bf16[16,256,128]{2,1,0:T(8,128)(2,1)S(1)}, u32[]{:S(2)}, u32[]{:S(2)}) %all-to-all-start.1) | async-done | bytes 1048608 | tf_op jit(solution)/shard_map/cond/branch_0_fun/all_to_all | solution.py:307
  71.4 11.3 %all-to-all-start.2 = ((bf16[16,16,7680]{2,1,0:T(8,128)(2,1)}), bf16[16,16,7680]{2,1,0:T(8,128)(2,1)}, u32[]{:S(2)}, u32[]{:S(2)}) async-start(bf16[16,16,7680]{2,1,0:T(8,128)(2,1)} %bitcast.17), calls=%async_computation.2 | async-start | bytes 7864320 | tf_op jit(solution)/shard_map/cond/branch_0_fun/all_to_all | solution.py:307
  85.4 2.3 collective-permute-done.3
  89.0 167.1 %spatial.4.ref = bf16[16,256,128]{2,1,0:T(8,128)(2,1)S(1)} custom-call(s32[2]{0:T(128)S(1)} %pad_add_fusion.first_ref, bf16[16,256,128]{2,1,0:T(8,128)(2,1)S(1)} %all-to-all-done.1.refs_0_, bf16[16,256,256]{2,1,0:T(8,128)(2,1)S(1)} %all-to-all-done.refs_1_.refs_2_, bf16[16,256,256]{2,1,0:T(8,128)(2,1)S(1)} %all-to-all-done.refs_1_.refs_2_, ...), custom_call_target="tpu_custom_call" | custom-call | flops 134217728 | bytes 131072 | tf_op jit(solution)/shard_map/cond/branch_0_fun/spatial/pallas_call | solution.py:250
  257.6 3.3 %collective-permute-start.5 = (bf16[4,256,128]{2,1,0:T(8,128)(2,1)S(1)}, bf16[4,256,128]{2,1,0:T(8,128)(2,1)S(1)}, u32[]{:S(2)}, u32[]{:S(2)}) collective-permute-start(bf16[4,256,128]{2,1,0:T(8,128)(2,1)S(1)} %get-tuple-element.45), channel_id=1, source_target_pairs={{0,8},{4,12},{8,0},{12,4},{1,9},{5,13},{9,1},{13,5},{2,10},{6,14},... | collective-permute-start | bytes 786440 | tf_op jit(solution)/shard_map/cond/branch_0_fun/ppermute | solution.py:335
  261.0 6.8 %temporal.3 = bf16[16,16,2560]{2,1,0:T(8,128)(2,1)} custom-call(bf16[16,16,7680]{2,1,0:T(8,128)(2,1)} %all-to-all-done.2.q_ref.k_ref.v_ref, bf16[16,16,7680]{2,1,0:T(8,128)(2,1)} %all-to-all-done.2.q_ref.k_ref.v_ref, bf16[16,16,7680]{2,1,0:T(8,128)(2,1)} %all-to-all-done.2.q_ref.k_ref.v_ref), custom_call_target="tpu_custom_call" | custom-call | flops 671088640 | bytes 5242880 | tf_op jit(solution)/shard_map/cond/branch_0_fun/temporal/pallas_call | solution.py:286
  267.8 5.0 %collective-permute-done.5.refs_2_ = bf16[4,256,128]{2,1,0:T(8,128)(2,1)S(1)} collective-permute-done((bf16[4,256,128]{2,1,0:T(8,128)(2,1)S(1)}, bf16[4,256,128]{2,1,0:T(8,128)(2,1)S(1)}, u32[]{:S(2)}, u32[]{:S(2)}) %collective-permute-start.5) | collective-permute-done | bytes 262176 | tf_op jit(solution)/shard_map/cond/branch_0_fun/ppermute | solution.py:335
  274.3 6.5 %all-to-all-start.3 = ((bf16[16,16,2560]{2,1,0:T(8,128)(2,1)}), bf16[16,16,2560]{2,1,0:T(8,128)(2,1)S(1)}, u32[]{:S(2)}, u32[]{:S(2)}) async-start(bf16[16,16,2560]{2,1,0:T(8,128)(2,1)} %temporal.3), calls=%async_computation.3 | async-start | bytes 2621440 | tf_op jit(solution)/shard_map/cond/branch_0_fun/all_to_all | solution.py:307
  280.8 2.8 collective-permute-start.8
  283.9 5.7 %collective-permute-done.7.refs_1_ = bf16[4,256,128]{2,1,0:T(8,128)(2,1)S(1)} collective-permute-done((bf16[4,256,128]{2,1,0:T(8,128)(2,1)S(1)}, bf16[4,256,128]{2,1,0:T(8,128)(2,1)S(1)}, u32[]{:S(2)}, u32[]{:S(2)}) %collective-permute-start.7) | collective-permute-done | bytes 262176 | tf_op jit(solution)/shard_map/cond/branch_0_fun/ppermute | solution.py:335
  289.6 5.7 %collective-permute-done.8.refs_2_ = bf16[4,256,128]{2,1,0:T(8,128)(2,1)S(1)} collective-permute-done((bf16[4,256,128]{2,1,0:T(8,128)(2,1)S(1)}, bf16[4,256,128]{2,1,0:T(8,128)(2,1)S(1)}, u32[]{:S(2)}, u32[]{:S(2)}) %collective-permute-start.8) | collective-permute-done | bytes 262176 | tf_op jit(solution)/shard_map/cond/branch_0_fun/ppermute | solution.py:335
  297.0 1.5 all-to-all-done.3
  298.5 2.7 unpack.3
  (27 shorter events, 13.1 us)
Async XLA Ops:
  6.4 1.3 copy-start.7
  7.8 6.9 %copy-start.26 = (s32[32]{0:T(128)S(1)}, s32[32]{0:T(128)}, u32[]{:S(2)}) copy-start(s32[32]{0:T(128)} %get-tuple-element.32.kind_ref) | copy-start | bytes 388 | tf_op jit(solution)/shard_map/cond
  7.8 37.4 %all-to-all-start = ((bf16[16,256,256]{2,1,0:T(8,128)(2,1)}), bf16[16,256,256]{2,1,0:T(8,128)(2,1)S(1)}, u32[]{:S(2)}, u32[]{:S(2)}) async-start(bf16[16,256,256]{2,1,0:T(8,128)(2,1)} %copy-done.7), calls=%async_computation | async-start | bytes 4194304 | tf_op jit(solution)/shard_map/cond/branch_0_fun/all_to_all | solution.py:307
  19.1 1.9 copy-start.11
  21.0 1.0 copy-start.15
  46.2 9.4 %collective-permute-start = (bf16[8,256,256]{2,1,0:T(8,128)(2,1)}, bf16[8,256,256]{2,1,0:T(8,128)(2,1)}, u32[]{:S(2)}, u32[]{:S(2)}) collective-permute-start(bf16[8,256,256]{2,1,0:T(8,128)(2,1)} %slice.8), channel_id=1, source_target_pairs={{0,32},{8,40},{1,33},{9,41},{2,34},{10,42},{3,35},{11,43},{4,36},{... | collective-permute-start | bytes 3145736 | tf_op jit(solution)/shard_map/cond/branch_0_fun/ppermute | solution.py:315
  47.8 7.7 %collective-permute-start.1 = (bf16[8,256,256]{2,1,0:T(8,128)(2,1)}, bf16[8,256,256]{2,1,0:T(8,128)(2,1)}, u32[]{:S(2)}, u32[]{:S(2)}) collective-permute-start(bf16[8,256,256]{2,1,0:T(8,128)(2,1)} %slice.8), channel_id=1, source_target_pairs={{0,64},{8,72},{1,65},{9,73},{2,66},{10,74},{3,67},{11,75},{4,68},{... | collective-permute-start | bytes 3145736 | tf_op jit(solution)/shard_map/cond/branch_0_fun/ppermute | solution.py:315
  49.5 6.0 %collective-permute-start.2 = (bf16[8,256,256]{2,1,0:T(8,128)(2,1)}, bf16[8,256,256]{2,1,0:T(8,128)(2,1)}, u32[]{:S(2)}, u32[]{:S(2)}) collective-permute-start(bf16[8,256,256]{2,1,0:T(8,128)(2,1)} %slice.8), channel_id=1, source_target_pairs={{0,96},{8,104},{1,97},{9,105},{2,98},{10,106},{3,99},{11,107},{4,1... | collective-permute-start | bytes 3145736 | tf_op jit(solution)/shard_map/cond/branch_0_fun/ppermute | solution.py:315
  51.2 20.2 %all-to-all-start.1 = ((bf16[16,256,128]{2,1,0:T(8,128)(2,1)}), bf16[16,256,128]{2,1,0:T(8,128)(2,1)S(1)}, u32[]{:S(2)}, u32[]{:S(2)}) async-start(bf16[16,256,128]{2,1,0:T(8,128)(2,1)} %copy-done.15), calls=%async_computation.1 | async-start | bytes 2097152 | tf_op jit(solution)/shard_map/cond/branch_0_fun/all_to_all | solution.py:307
  71.4 189.6 %all-to-all-start.2 = ((bf16[16,16,7680]{2,1,0:T(8,128)(2,1)}), bf16[16,16,7680]{2,1,0:T(8,128)(2,1)}, u32[]{:S(2)}, u32[]{:S(2)}) async-start(bf16[16,16,7680]{2,1,0:T(8,128)(2,1)} %bitcast.17), calls=%async_computation.2 | async-start | bytes 7864320 | tf_op jit(solution)/shard_map/cond/branch_0_fun/all_to_all | solution.py:307
  82.8 4.9 %collective-permute-start.3 = (bf16[8,256,256]{2,1,0:T(8,128)(2,1)}, bf16[8,256,256]{2,1,0:T(8,128)(2,1)}, u32[]{:S(2)}, u32[]{:S(2)}) collective-permute-start(bf16[8,256,256]{2,1,0:T(8,128)(2,1)} %select_select_fusion), channel_id=1, source_target_pairs={{0,16},{8,24},{32,48},{40,56},{64,80},{72,88},{96,112},{104,120},{... | collective-permute-start | bytes 3145736 | tf_op jit(solution)/shard_map/cond/branch_0_fun/ppermute | solution.py:315
  256.2 11.6 %collective-permute-start.4 = (bf16[4,256,128]{2,1,0:T(8,128)(2,1)S(1)}, bf16[4,256,128]{2,1,0:T(8,128)(2,1)S(1)}, u32[]{:S(2)}, u32[]{:S(2)}) collective-permute-start(bf16[4,256,128]{2,1,0:T(8,128)(2,1)S(1)} %get-tuple-element.44), channel_id=1, source_target_pairs={{0,4},{4,8},{8,12},{12,0},{1,5},{5,9},{9,13},{13,1},{2,6},{6,10},{... | collective-permute-start | bytes 786440 | tf_op jit(solution)/shard_map/cond/branch_0_fun/ppermute | solution.py:335
  257.6 15.2 %collective-permute-start.5 = (bf16[4,256,128]{2,1,0:T(8,128)(2,1)S(1)}, bf16[4,256,128]{2,1,0:T(8,128)(2,1)S(1)}, u32[]{:S(2)}, u32[]{:S(2)}) collective-permute-start(bf16[4,256,128]{2,1,0:T(8,128)(2,1)S(1)} %get-tuple-element.45), channel_id=1, source_target_pairs={{0,8},{4,12},{8,0},{12,4},{1,9},{5,13},{9,1},{13,5},{2,10},{6,14},... | collective-permute-start | bytes 786440 | tf_op jit(solution)/shard_map/cond/branch_0_fun/ppermute | solution.py:335
  260.9 11.9 %collective-permute-start.6 = (bf16[4,256,128]{2,1,0:T(8,128)(2,1)S(1)}, bf16[4,256,128]{2,1,0:T(8,128)(2,1)S(1)}, u32[]{:S(2)}, u32[]{:S(2)}) collective-permute-start(bf16[4,256,128]{2,1,0:T(8,128)(2,1)S(1)} %get-tuple-element.46), channel_id=1, source_target_pairs={{0,12},{4,0},{8,4},{12,8},{1,13},{5,1},{9,5},{13,9},{2,14},{6,2},{... | collective-permute-start | bytes 786440 | tf_op jit(solution)/shard_map/cond/branch_0_fun/ppermute | solution.py:335
  274.3 24.2 %all-to-all-start.3 = ((bf16[16,16,2560]{2,1,0:T(8,128)(2,1)}), bf16[16,16,2560]{2,1,0:T(8,128)(2,1)S(1)}, u32[]{:S(2)}, u32[]{:S(2)}) async-start(bf16[16,16,2560]{2,1,0:T(8,128)(2,1)} %temporal.3), calls=%async_computation.3 | async-start | bytes 2621440 | tf_op jit(solution)/shard_map/cond/branch_0_fun/all_to_all | solution.py:307
  280.8 8.7 %collective-permute-start.7 = (bf16[4,256,128]{2,1,0:T(8,128)(2,1)S(1)}, bf16[4,256,128]{2,1,0:T(8,128)(2,1)S(1)}, u32[]{:S(2)}, u32[]{:S(2)}) collective-permute-start(bf16[4,256,128]{2,1,0:T(8,128)(2,1)S(1)} %get-tuple-element.59), channel_id=1, source_target_pairs={{0,1},{1,2},{2,3},{3,0},{4,5},{5,6},{6,7},{7,4},{8,9},{9,10},{10,1... | collective-permute-start | bytes 786440 | tf_op jit(solution)/shard_map/cond/branch_0_fun/ppermute | solution.py:335
  280.8 14.5 %collective-permute-start.8 = (bf16[4,256,128]{2,1,0:T(8,128)(2,1)S(1)}, bf16[4,256,128]{2,1,0:T(8,128)(2,1)S(1)}, u32[]{:S(2)}, u32[]{:S(2)}) collective-permute-start(bf16[4,256,128]{2,1,0:T(8,128)(2,1)S(1)} %get-tuple-element.60), channel_id=1, source_target_pairs={{0,2},{1,3},{2,0},{3,1},{4,6},{5,7},{6,4},{7,5},{8,10},{9,11},{10,... | collective-permute-start | bytes 786440 | tf_op jit(solution)/shard_map/cond/branch_0_fun/ppermute | solution.py:335
  283.6 11.9 %collective-permute-start.9 = (bf16[4,256,128]{2,1,0:T(8,128)(2,1)S(1)}, bf16[4,256,128]{2,1,0:T(8,128)(2,1)S(1)}, u32[]{:S(2)}, u32[]{:S(2)}) collective-permute-start(bf16[4,256,128]{2,1,0:T(8,128)(2,1)S(1)} %get-tuple-element.61), channel_id=1, source_target_pairs={{0,3},{1,0},{2,1},{3,2},{4,7},{5,4},{6,5},{7,6},{8,11},{9,8},{10,9... | collective-permute-start | bytes 786440 | tf_op jit(solution)/shard_map/cond/branch_0_fun/ppermute | solution.py:335
